TPU v7x, 32 devices: a whole 2x2x4 slice. The times are simulated.
32 devices in a mesh: case: 2 (over y), blk: 4 (over z), split: 2 (over x), sub: 2 (over core).
Axes of the slice: x: 2, y: 2, z: 4, core: 2. Of those that a mesh axis runs over, the one named last changes fastest.
Arguments:
- cell_series: bfloat16 [32768, 4, 512], P(('case', 'blk', 'split', 'sub')), parts along dimension 0, may hold values from -6 to 6
- cell_count: int32 [32], P(('case', 'blk', 'split', 'sub')), parts along dimension 0, may hold values from 768 to 1024, as said below
- cell_target: int32 [32768], P(('case', 'blk', 'split', 'sub')), parts along dimension 0, may hold values from 0 to 2047, as said below
- surface: float32 [4, 8192], P(None, ('case', 'blk', 'split', 'sub')), parts along dimension 1, may hold values from -8.5 to 16.5, as said below
- observers: float32 [3, 1024], P(None, 'case'), parts along dimension 1, may hold values from -45 to 53, as said below
Outputs:
- pressure: float32 [1024, 2, 8], P(('case', 'blk')), parts along dimension 0
There are 2 independent parts, one for each index of `case`. A program takes and returns all parts, laid end to end along the dimension named above; each array names one. Nothing has to cross between parts.
Inputs may be any that keep to these rules, and one draw needn't show every extreme that they name: Cells i of a device with i < cell_count are live. `cell_target`: an entry t names local surface point t mod 256 of the device whose index along blk+split is t // 256 and whose sub index is the cell's. Among the rows of one device no such owner is named more than 192 times; in every device one owner is named by exactly 192 live rows, the same owner for all devices of one sub index. Every surface point lies within 8.5 of the point (8, 0, 0); panel areas are positive. `observers`: every observer lies 18 or more from the point (8, 0, 0).
All inputs are finite; a program needn't handle non-finite values.
Results may differ from a plain program's by a relative error of at most 0.0027.
Values may be sent and summed in bfloat16 or wider, within the bound.
A program may use at most 64 MiB of HBM per device.

v0:
```python
import math

import jax
import jax.numpy as jnp
from jax import lax
from jax.sharding import PartitionSpec as P

NF = 8


def spectral_lookup_matrix(signal_readings):
    clock_moments = jnp.arange(signal_readings, dtype=jnp.int32)
    spectral_slot_number = jnp.arange(NF, dtype=jnp.int32) + signal_readings // 16
    modulo_angle_value = spectral_slot_number[:, None] * clock_moments[None, :] % signal_readings
    phases = 2.0 * math.pi / signal_readings * modulo_angle_value.astype(jnp.float32)
    hann_attenuation_curve = 0.5 - 0.5 * jnp.cos(
        2.0 * math.pi / signal_readings * clock_moments.astype(jnp.float32)
    )
    scaled = 2.0 / signal_readings * hann_attenuation_curve[None, :]
    return jnp.concatenate([scaled * jnp.cos(phases), -scaled * jnp.sin(phases)], axis=0).astype(
        jnp.bfloat16
    )


def radiate(spectra, surface, listeners, amplitude):
    delta_x = listeners[0][:, None] - surface[0][None, :]
    delta_y = listeners[1][:, None] - surface[1][None, :]
    delta_z = listeners[2][:, None] - surface[2][None, :]
    radius = jnp.sqrt(delta_x * delta_x + delta_y * delta_y + delta_z * delta_z)
    inverse = 1.0 / radius
    normal_x = delta_x * inverse
    normal_y = delta_y * inverse
    normal_z = delta_z * inverse
    quadrature_factor = surface[3][None, :] * inverse * (amplitude / (4.0 * math.pi))
    blocks = spectra.reshape(2, NF, 4, spectra.shape[1])
    real_list = []
    imag_list = []
    for harmonic in range(NF):
        wavenumber = 0.5 + 0.25 * harmonic
        real_part = blocks[0, harmonic]
        imag_part = blocks[1, harmonic]
        load_real = (
            real_part[1][None, :] * normal_x
            + real_part[2][None, :] * normal_y
            + real_part[3][None, :] * normal_z
        )
        load_imag = (
            imag_part[1][None, :] * normal_x
            + imag_part[2][None, :] * normal_y
            + imag_part[3][None, :] * normal_z
        )
        source_real = (
            -wavenumber * imag_part[0][None, :] + load_real * inverse - wavenumber * load_imag
        )
        source_imag = (
            wavenumber * real_part[0][None, :] + wavenumber * load_real + load_imag * inverse
        )
        cosine = jnp.cos(wavenumber * radius)
        sinusoid = jnp.sin(wavenumber * radius)
        real_list.append(
            jnp.sum(quadrature_factor * (source_real * cosine + source_imag * sinusoid), axis=1)
        )
        imag_list.append(
            jnp.sum(quadrature_factor * (source_imag * cosine - source_real * sinusoid), axis=1)
        )
    real_out = jnp.stack(real_list, axis=1)
    imag_out = jnp.stack(imag_list, axis=1)
    return jnp.stack([real_out, imag_out], axis=1)


def local(cell_series, cell_count, cell_target, surface, observers):
    rows_dev = cell_series.shape[0]
    signal_readings = cell_series.shape[2]
    points_dev = surface.shape[1]
    source_groups = lax.axis_size("blk") * lax.axis_size("split")
    devices = source_groups * lax.axis_size("sub")
    capacity = (3 * rows_dev + 2 * source_groups - 1) // (2 * source_groups)
    slot_total = source_groups * capacity
    amplitude = 150.0 * math.sqrt(
        signal_readings * points_dev / (rows_dev * (points_dev * devices))
    )
    twiddle = spectral_lookup_matrix(signal_readings)
    row_index = jnp.arange(rows_dev, dtype=jnp.int32)
    active = row_index < cell_count[0]
    owner_index = cell_target // points_dev
    point_index = cell_target % points_dev
    matches = (
        (owner_index[:, None] == jnp.arange(source_groups, dtype=jnp.int32)[None, :])
        & active[:, None]
    ).astype(jnp.int32)
    sorted_ranking = jnp.sum(jnp.cumsum(matches, axis=0) * matches, axis=1) - 1
    destination = jnp.where(active, owner_index * capacity + sorted_ranking, slot_total)
    slot_source = (
        jnp.full((slot_total + 1,), rows_dev, jnp.int32).at[destination].set(row_index)[:slot_total]
    )
    slot_point = jnp.take(point_index, slot_source, mode="fill", fill_value=-1)
    flattened = cell_series.reshape(rows_dev * 4, signal_readings)
    per_cell = jnp.einsum("jt,rt->jr", twiddle, flattened, preferred_element_type=jnp.float32)
    per_cell = per_cell.reshape(2 * NF, rows_dev, 4).transpose(1, 0, 2).reshape(rows_dev, 8 * NF)
    outgoing = jnp.take(per_cell, slot_source, axis=0, mode="fill", fill_value=0.0)
    arrived_points, arrived = (
        lax.all_to_all(
            slot_point.reshape(source_groups, capacity),
            ("blk", "split"),
            split_axis=0,
            concat_axis=0,
            tiled=True,
        ),
        lax.all_to_all(
            outgoing.reshape(source_groups, capacity, 8 * NF),
            ("blk", "split"),
            split_axis=0,
            concat_axis=0,
            tiled=True,
        ),
    )
    arrived_points = arrived_points.reshape(slot_total)
    placing = (arrived_points[:, None] == jnp.arange(points_dev, dtype=jnp.int32)[None, :]).astype(
        jnp.float32
    )
    spectra = jnp.dot(
        arrived.reshape(slot_total, 8 * NF).T,
        placing,
        precision=lax.Precision.HIGHEST,
        preferred_element_type=jnp.float32,
    )
    summed = lax.psum_scatter(
        radiate(spectra, surface, observers, amplitude), "blk", scatter_dimension=0, tiled=True
    )
    return lax.psum(summed, ("split", "sub"))


def solution(mesh):
    return jax.shard_map(
        local,
        mesh=mesh,
        in_specs=(
            P(("case", "blk", "split", "sub"), None, None),
            P(("case", "blk", "split", "sub")),
            P(("case", "blk", "split", "sub")),
            P(None, ("case", "blk", "split", "sub")),
            P(None, "case"),
        ),
        out_specs=P(("case", "blk"), None, None),
        check_vma=False,
    )
```

profile of v0, /device:TPU:0, one launch (start us, length us, event | category | flops | bytes accessed | tf_op | source)
XLA Modules:
  0.0 115.6 jit_solution(8116364706808095267)
XLA Ops:
  6.5 0.7 add_select_fusion.1
  7.9 2.3 %reduce-window.6 = s32[8,8,128]{2,1,0:T(8,128)S(1)} reduce-window(s32[8,8,128]{2,1,0:T(8,128)S(1)} %fusion.62, s32[]{:T(128)} %constant.50.clone.1), window={size=1x1x128 pad=0_0x0_0x127_0}, to_apply=%region_0.1 | reduce-window | flops 1040384 | bytes 65540 | tf_op jit(solution)/shard_map/reduce-window
  10.8 4.3 %scatter_custom_fusion = s32[1537]{0:T(1024)S(1)} fusion(s32[1024]{0:T(1024)S(1)} %compare_select_fusion.3, s32[1024]{0:T(1024)S(1)} %iota.57, s32[]{:T(128)} %constant.46.clone.1), kind=kCustom, calls=%fused_computation.159 | custom fusion | bytes 6152 | tf_op jit(solution)/shard_map/scatter | solution.py:94
  15.1 5.9 %gather_fusion.1 = s32[1536]{0:T(1024)S(1)} fusion(s32[1024]{0:T(1024)S(1)} %get-tuple-element.94, s32[2048]{0:T(1024)S(1)} %pad_clamp_fusion), kind=kCustom, calls=%fused_computation.1 | custom fusion | bytes 18432 | tf_op jit(solution)/shard_map/jit(_take)/gather | solution.py:96
  21.1 0.6 and_select_fusion
  21.8 7.3 %all-to-all-start.1 = ((s32[8,1,192]{2,1,0:T(1,128)}), s32[8,1,192]{2,1,0:T(1,128)S(1)}, u32[]{:S(2)}, u32[]{:S(2)}) async-start(s32[8,1,192]{2,1,0:T(1,128)} %and_select_fusion), calls=%async_computation.1 | async-start | bytes 16384 | tf_op jit(solution)/shard_map/all_to_all | solution.py:102
  29.3 3.4 %fusion.5 = f32[1024,16,4]{0,1,2:T(8,128)S(1)} fusion(bf16[1024,4,512]{2,1,0:T(4,128)(2,1)} %param.5, bf16[8,512]{1,0:T(8,128)(2,1)S(1)} %get-tuple-element.97, bf16[8,512]{1,0:T(8,128)(2,1)S(1)} %get-tuple-element.96), kind=kOutput, calls=%fused_computation.8 | convolution fusion | flops 67141632 | bytes 4472832 | tf_op jit(solution)/shard_map/jt,rt->jr/dot_general | solution.py:98
  33.2 2.6 %gather_fusion = f32[1536,64]{1,0:T(8,128)S(1)} fusion(f32[1024,64]{1,0:T(8,128)S(1)} %copy.23, s32[2048]{0:T(1024)S(1)} %pad_clamp_fusion), kind=kCustom, calls=%fused_computation | custom fusion | bytes 792576 | tf_op jit(solution)/shard_map/jit(_take)/gather | solution.py:100
  35.8 0.3 copy.24
  36.2 0.8 broadcast_select_fusion
  37.0 6.0 %all-to-all-start = ((f32[8,192,64]{1,2,0:T(8,128)}), f32[8,192,64]{1,2,0:T(8,128)S(1)}, u32[]{:S(2)}, u32[]{:S(2)}) async-start(f32[8,192,64]{1,2,0:T(8,128)} %broadcast_select_fusion), calls=%async_computation | async-start | bytes 1048576 | tf_op jit(solution)/shard_map/all_to_all | solution.py:109
  43.2 13.8 %all-to-all-done = f32[8,192,64]{1,2,0:T(8,128)S(1)} async-done(((f32[8,192,64]{1,2,0:T(8,128)}), f32[8,192,64]{1,2,0:T(8,128)S(1)}, u32[]{:S(2)}, u32[]{:S(2)}) %all-to-all-start) | async-done | bytes 393248 | tf_op jit(solution)/shard_map/all_to_all | solution.py:109
  57.6 0.8 fusion.3
  58.5 3.3 %multiply_reduce_fusion.8 = (f32[512]{0:T(512)S(1)}, f32[512]{0:T(512)S(1)}) fusion(f32[256]{0:T(256)S(1)} %bitcast.252, f32[512]{0:T(512)S(1)} %bitcast.156, f32[256]{0:T(256)S(1)} %bitcast.260, f32[512]{0:T(512)S(1)} %bitcast.164, f32[256]{0:T(256)S(1)} %bitcast.244, f32[512]{0:T(512)S(1)} %bitcast.148, f32[256]{0:T(256)S(1)} %bitcast.229, ...), kind=kLoop, calls=%fused_computation.27 | loop fusion | flops 5635072 | bytes 22528 | tf_op jit(solution)/shard_map/reduce_sum | solution.py:61
  61.8 3.1 %multiply_reduce_fusion.9 = (f32[512]{0:T(512)S(1)}, f32[512]{0:T(512)S(1)}) fusion(f32[256]{0:T(256)S(1)} %bitcast.253, f32[512]{0:T(512)S(1)} %bitcast.157, f32[256]{0:T(256)S(1)} %bitcast.261, f32[512]{0:T(512)S(1)} %bitcast.165, f32[256]{0:T(256)S(1)} %bitcast.245, f32[512]{0:T(512)S(1)} %bitcast.149, f32[256]{0:T(256)S(1)} %bitcast.221, ...), kind=kLoop, calls=%fused_computation.32 | loop fusion | flops 5635072 | bytes 22528 | tf_op jit(solution)/shard_map/reduce_sum | solution.py:61
  64.9 3.1 %multiply_reduce_fusion.10 = (f32[512]{0:T(512)S(1)}, f32[512]{0:T(512)S(1)}) fusion(f32[256]{0:T(256)S(1)} %bitcast.254, f32[512]{0:T(512)S(1)} %bitcast.158, f32[256]{0:T(256)S(1)} %bitcast.262, f32[512]{0:T(512)S(1)} %bitcast.166, f32[256]{0:T(256)S(1)} %bitcast.246, f32[512]{0:T(512)S(1)} %bitcast.150, f32[256]{0:T(256)S(1)} %bitcast.213, ...), kind=kLoop, calls=%fused_computation.37 | loop fusion | flops 5635072 | bytes 22528 | tf_op jit(solution)/shard_map/reduce_sum | solution.py:61
  68.0 3.1 %multiply_reduce_fusion.11 = (f32[512]{0:T(512)S(1)}, f32[512]{0:T(512)S(1)}) fusion(f32[256]{0:T(256)S(1)} %bitcast.255, f32[512]{0:T(512)S(1)} %bitcast.159, f32[256]{0:T(256)S(1)} %bitcast.263, f32[512]{0:T(512)S(1)} %bitcast.167, f32[256]{0:T(256)S(1)} %bitcast.247, f32[512]{0:T(512)S(1)} %bitcast.151, f32[256]{0:T(256)S(1)} %bitcast.205, ...), kind=kLoop, calls=%fused_computation.82 | loop fusion | flops 5635072 | bytes 22528 | tf_op jit(solution)/shard_map/reduce_sum | solution.py:61
  71.1 3.1 %multiply_reduce_fusion.12 = (f32[512]{0:T(512)S(1)}, f32[512]{0:T(512)S(1)}) fusion(f32[256]{0:T(256)S(1)} %bitcast.256, f32[512]{0:T(512)S(1)} %bitcast.160, f32[256]{0:T(256)S(1)} %bitcast.264, f32[512]{0:T(512)S(1)} %bitcast.168, f32[256]{0:T(256)S(1)} %bitcast.248, f32[512]{0:T(512)S(1)} %bitcast.152, f32[256]{0:T(256)S(1)} %bitcast.197, ...), kind=kLoop, calls=%fused_computation.85 | loop fusion | flops 5635072 | bytes 22528 | tf_op jit(solution)/shard_map/reduce_sum | solution.py:61
  74.2 3.0 %multiply_reduce_fusion.13 = (f32[512]{0:T(512)S(1)}, f32[512]{0:T(512)S(1)}) fusion(f32[256]{0:T(256)S(1)} %bitcast.257, f32[512]{0:T(512)S(1)} %bitcast.161, f32[256]{0:T(256)S(1)} %bitcast.265, f32[512]{0:T(512)S(1)} %bitcast.169, f32[256]{0:T(256)S(1)} %bitcast.249, f32[512]{0:T(512)S(1)} %bitcast.153, f32[256]{0:T(256)S(1)} %bitcast.189, ...), kind=kLoop, calls=%fused_computation.88 | loop fusion | flops 5241856 | bytes 22528 | tf_op jit(solution)/shard_map/reduce_sum | solution.py:61
  77.2 3.1 %multiply_reduce_fusion.14 = (f32[512]{0:T(512)S(1)}, f32[512]{0:T(512)S(1)}) fusion(f32[256]{0:T(256)S(1)} %bitcast.258, f32[512]{0:T(512)S(1)} %bitcast.162, f32[256]{0:T(256)S(1)} %bitcast.266, f32[512]{0:T(512)S(1)} %bitcast.170, f32[256]{0:T(256)S(1)} %bitcast.250, f32[512]{0:T(512)S(1)} %bitcast.154, f32[256]{0:T(256)S(1)} %bitcast.181, ...), kind=kLoop, calls=%fused_computation.91 | loop fusion | flops 5635072 | bytes 22528 | tf_op jit(solution)/shard_map/reduce_sum | solution.py:61
  80.3 3.1 %multiply_reduce_fusion.15 = (f32[512]{0:T(512)S(1)}, f32[512]{0:T(512)S(1)}) fusion(f32[256]{0:T(256)S(1)} %bitcast.259, f32[512]{0:T(512)S(1)} %bitcast.163, f32[256]{0:T(256)S(1)} %bitcast.267, f32[512]{0:T(512)S(1)} %bitcast.171, f32[256]{0:T(256)S(1)} %bitcast.251, f32[512]{0:T(512)S(1)} %bitcast.155, f32[256]{0:T(256)S(1)} %bitcast.173, ...), kind=kLoop, calls=%fused_computation.94 | loop fusion | flops 5635072 | bytes 22528 | tf_op jit(solution)/shard_map/reduce_sum | solution.py:61
  83.5 0.6 pad_maximum_fusion
  84.1 18.1 %reduce-scatter.2.cloned.1.call-done = f32[128,2,8]{0,2,1:T(8,128)} async-done(((f32[512,2,8]{0,2,1:T(8,128)}), f32[128,2,8]{0,2,1:T(8,128)}) %reduce-scatter.2.cloned.1.call-update) | async-done | bytes 8208 | tf_op jit(solution)/shard_map/reduce_scatter | solution.py:127
  102.3 6.4 %psum.7 = f32[128,2,8]{0,2,1:T(8,128)} all-reduce(f32[128,2,8]{0,2,1:T(8,128)} %reduce-scatter.2.cloned.1.call-done), channel_id=1, replica_groups=mesh['case'=2,'blk'=4,'split'=2,'sub'=2] {'split','sub'}, use_global_device_ids=true, to_apply=%region_21.22 | all-reduce | flops 2048 | bytes 16384 | tf_op jit(solution)/shard_map/psum | solution.py:130
  (41 shorter events, 2.4 us)
Async XLA Ops:
  21.8 15.2 %all-to-all-start.1 = ((s32[8,1,192]{2,1,0:T(1,128)}), s32[8,1,192]{2,1,0:T(1,128)S(1)}, u32[]{:S(2)}, u32[]{:S(2)}) async-start(s32[8,1,192]{2,1,0:T(1,128)} %and_select_fusion), calls=%async_computation.1 | async-start | bytes 16384 | tf_op jit(solution)/shard_map/all_to_all | solution.py:102
  33.2 9.9 %copy-start.1 = (f32[4,256]{1,0:T(4,128)S(1)}, f32[4,256]{1,0:T(4,128)}, u32[]{:S(2)}) copy-start(f32[4,256]{1,0:T(4,128)} %param.8) | copy-start | bytes 12292
  33.2 9.9 %copy-start = (f32[3,512]{1,0:T(4,128)S(1)}, f32[3,512]{1,0:T(4,128)}, u32[]{:S(2)}) copy-start(f32[3,512]{1,0:T(4,128)} %param.9) | copy-start | bytes 18436
  37.0 20.0 %all-to-all-start = ((f32[8,192,64]{1,2,0:T(8,128)}), f32[8,192,64]{1,2,0:T(8,128)S(1)}, u32[]{:S(2)}, u32[]{:S(2)}) async-start(f32[8,192,64]{1,2,0:T(8,128)} %broadcast_select_fusion), calls=%async_computation | async-start | bytes 1048576 | tf_op jit(solution)/shard_map/all_to_all | solution.py:109
  43.0 59.3 %reduce-scatter.2.cloned.1.call-start = ((), (), s32[]{:S(2)}) async-start(), calls=%async_computation.3 | async-start | bytes 40960 | tf_op jit(solution)/shard_map/reduce_scatter | solution.py:127
Sparse Core Ops, SparseCore 0:
  84.3 17.9 reduce-scatter.1
where the time goes:
time: 116 us
  waiting for transfers between devices  31.9 us (28%)
  other arithmetic  30.6 us (26%)
  local copies, waits for them, and re-layouts  14.8 us (13%)
  between operations  14.3 us (12%)
  starting transfers between devices  13.3 us (11%)
  blocking collectives  6.44 us (6%)
  matrix products  4.22 us (4%)
    reduce_sum x8, other arithmetic, radiate(): jnp.sum(quadrature_factor * (source_real * cosine + source_imag * sinusoi...  24.9 us
    reduce_scatter x1, waiting for transfers between devices, local(): lax.psum_scatter(radiate(spectra, surface, observers, amplitude), 'blk',...  18.1 us
    all_to_all x1, waiting for transfers between devices, local(): lax.all_to_all(outgoing.reshape(source_groups, capacity, 8 * NF), ('blk',...  13.8 us
    all_to_all x1, starting transfers between devices, local(): lax.all_to_all(slot_point.reshape(source_groups, capacity), ('blk', 'spli...  7.25 us
    psum x1, blocking collectives, local(): return lax.psum(summed, ('split', 'sub'))  6.44 us
    all_to_all x1, starting transfers between devices, local(): lax.all_to_all(outgoing.reshape(source_groups, capacity, 8 * NF), ('blk',...  6 us
    gather x2, local copies, waits for them, and re-layouts, local(): slot_point = jnp.take(point_index, slot_source, mode='fill', fill_value=-1)  5.93 us
    scatter x1, local copies, waits for them, and re-layouts, local(): jnp.full((slot_total + 1,), rows_dev, jnp.int32).at[destination]  4.32 us
  transfers between devices with their start and end apart: 3, of which 2 were waited for; matrix products, arithmetic and copies ran while one was open for 7% of the time, Pallas kernels for 0%

commit v1 on v0

v1 whole, which is shorter than its diff:
```python
import math

import jax
import jax.numpy as jnp
from jax import lax
from jax.experimental import pallas as pl
from jax.experimental.pallas import tpu as pltpu
from jax.sharding import PartitionSpec as P

NF = 8
MESH = pl.DeviceIdType.MESH


def polynomials(terms):
    import numpy as np

    nodes = np.cos((np.arange(400) + 0.5) * np.pi / 400)
    squares = (nodes + 1.0) * 0.125
    u = np.sqrt(squares)
    out = []
    for values in (np.sin(2 * np.pi * u) / u, np.cos(2 * np.pi * u)):
        series = np.polynomial.chebyshev.chebfit(nodes, values, terms - 1)
        powers = np.polynomial.chebyshev.cheb2poly(series)
        total = np.zeros(1)
        for a in powers[::-1]:
            total = np.polynomial.polynomial.polyadd(
                np.polynomial.polynomial.polymul(total, [-1.0, 8.0]), [a]
            )
        out.append([float(np.float32(c)) for c in total[:terms]])
    return out


def spectral_lookup_matrix(signal_readings):
    clock_moments = jnp.arange(signal_readings, dtype=jnp.int32)
    spectral_slot_number = jnp.arange(NF, dtype=jnp.int32) + signal_readings // 16
    modulo_angle_value = spectral_slot_number[:, None] * clock_moments[None, :] % signal_readings
    phases = 2.0 * math.pi / signal_readings * modulo_angle_value.astype(jnp.float32)
    hann_attenuation_curve = 0.5 - 0.5 * jnp.cos(
        2.0 * math.pi / signal_readings * clock_moments.astype(jnp.float32)
    )
    scaled = 2.0 / signal_readings * hann_attenuation_curve[None, :]
    return jnp.concatenate([scaled * jnp.cos(phases), -scaled * jnp.sin(phases)], axis=0).astype(
        jnp.bfloat16
    )


def horner(coefficients, v):
    total = coefficients[-1] * v + coefficients[-2]
    for c in coefficients[-3::-1]:
        total = total * v + c
    return total


def make_kernel(n_blk, n_split, n_sub, rows, points, n_obs, amplitude):
    groups = n_blk * n_split
    devices = groups * n_sub
    obs_blk = n_obs // n_blk
    sin_c, cos_c = polynomials(7)
    half = 256 if n_obs % 256 == 0 else n_obs
    step_q = 16

    def each(count, body):
        lax.fori_loop(1, count, lambda i, c: (body(i), c)[1], 0, unroll=count <= 16)

    def kernel(
        pc_ref, count_ref, target_ref, surface_ref, surface_t_ref, obs_ref, out_ref,
        stage, recv, green, rows_scr, out_scr, press, recv2,
        send_sem, recv_sem, send_sem2, recv_sem2,
    ):
        blk = lax.axis_index("blk")
        split = lax.axis_index("split")
        sub = lax.axis_index("sub")
        group = blk * n_split + split
        me = group * n_sub + sub

        def device(index):
            g = index // n_sub
            return {"blk": g // n_split, "split": g % n_split, "sub": index % n_sub}

        barrier = pltpu.get_barrier_semaphore()

        def greet(i):
            pl.semaphore_signal(
                barrier, inc=1, device_id=device(lax.rem(me + i, devices)), device_id_type=MESH
            )

        each(devices, greet)

        pc = pc_ref[...]
        high = pc.astype(jnp.bfloat16)
        low = (pc - high.astype(jnp.float32)).astype(jnp.bfloat16)
        both = jnp.concatenate([high, low], axis=0)
        live = lax.broadcasted_iota(jnp.int32, (1, rows), 1) < count_ref[0]
        target = jnp.where(live, target_ref[...], -1)
        point = lax.broadcasted_iota(jnp.int32, (points, rows), 0)

        def partial_sums(g):
            chosen = (point == target - g * points).astype(jnp.float32).astype(jnp.bfloat16)
            sums = lax.dot_general(
                both, chosen, (((1,), (1,)), ((), ())), preferred_element_type=jnp.float32
            )
            return (sums[: 8 * NF] + sums[8 * NF :]).astype(jnp.bfloat16)

        def spectra_copy(i):
            g = lax.rem(group + i, groups)
            return pltpu.make_async_remote_copy(
                src_ref=stage.at[i],
                dst_ref=recv.at[i],
                send_sem=send_sem.at[i],
                recv_sem=recv_sem.at[i],
                device_id={"blk": g // n_split, "split": g % n_split, "sub": sub},
                device_id_type=MESH,
            )

        pl.semaphore_wait(barrier, devices - 1)

        def send_spectra(i):
            stage[i] = partial_sums(lax.rem(group + i, groups))
            spectra_copy(i).start()

        each(groups, send_spectra)
        stage[0] = partial_sums(group)

        def green_step(step, carry):
            start = pl.multiple_of(step * step_q, step_q)
            at = surface_t_ref[pl.ds(start, step_q), :]
            for h in range(n_obs // half):
                lanes = pl.ds(h * half, half)
                d_x = obs_ref[0:1, lanes] - at[:, 0:1]
                d_y = obs_ref[1:2, lanes] - at[:, 1:2]
                d_z = obs_ref[2:3, lanes] - at[:, 2:3]
                square = d_x * d_x + d_y * d_y + d_z * d_z
                inverse = lax.rsqrt(square)
                radius = square * inverse
                turns = radius * (0.25 / (2.0 * math.pi))
                turns = turns - jnp.round(turns)
                v = turns * turns
                cosine = horner(cos_c, v)
                sine = horner(sin_c, v) * turns
                twice = cosine + cosine
                scale = inverse * inverse
                old_r = cosine * scale
                old_i = -sine * scale
                new_r = twice * old_r - scale
                new_i = twice * old_i
                for f in range(NF):
                    k = 0.5 + 0.25 * f
                    base = f * 4 * points + start
                    parts = (
                        new_r * radius,
                        new_i * radius,
                        new_r * inverse - k * new_i,
                        new_i * inverse + k * new_r,
                    )
                    for p, value in enumerate(parts):
                        green[pl.ds(base + p * points, step_q), lanes] = value.astype(jnp.bfloat16)
                    old_r, new_r = new_r, twice * new_r - old_r
                    old_i, new_i = new_i, twice * new_i - old_i
            return carry

        lax.fori_loop(0, points // step_q, green_step, 0)

        each(groups, lambda i: spectra_copy(i).wait_recv())
        if groups <= 16:
            spectra = stage[0].astype(jnp.float32)
            for i in range(1, groups):
                spectra += recv[i].astype(jnp.float32)
        else:
            spectra = lax.fori_loop(
                1, groups, lambda i, s: s + recv[i].astype(jnp.float32), stage[0].astype(jnp.float32)
            )
        surface = surface_ref[...]
        spectra = spectra * (surface[3:4] * (amplitude / (4.0 * math.pi)))
        wave = 0.5 + 0.25 * lax.broadcasted_iota(jnp.int32, (NF, points), 0).astype(jnp.float32)
        part = [
            (spectra[16 * c : 16 * c + NF], spectra[16 * c + NF : 16 * c + 2 * NF]) for c in range(4)
        ]
        mono_r = -wave * part[0][1]
        mono_i = wave * part[0][0]
        along_r = sum(surface[c : c + 1] * part[c + 1][0] for c in range(3))
        along_i = sum(surface[c : c + 1] * part[c + 1][1] for c in range(3))
        zero = jnp.zeros_like(wave)
        lines = [(mono_r, -mono_i, -along_r, along_i), (mono_i, mono_r, -along_i, -along_r)]
        for c in range(1, 4):
            r, i = part[c]
            lines.append((zero, zero, r, -i))
            lines.append((zero, zero, i, r))
        for t, line in enumerate(lines):
            for p, value in enumerate(line):
                for q in range(points // 128):
                    rows_scr[p * (points // 128) + q, t * NF : (t + 1) * NF, :] = value[
                        :, q * 128 : (q + 1) * 128
                    ]
        for f in range(NF):
            left = jnp.concatenate(
                [
                    rows_scr[p, pl.ds(f, 8, stride=NF), :]
                    for p in range(4 * points // 128)
                ],
                axis=1,
            )
            left_high = left.astype(jnp.bfloat16).astype(jnp.float32)
            left = jnp.concatenate([left_high, left - left_high], axis=0).astype(jnp.bfloat16)
            result = jnp.dot(
                left,
                green[f * 4 * points : (f + 1) * 4 * points, :],
                preferred_element_type=jnp.float32,
            )
            result = result[:8] + result[8:]
            for q in range(n_obs // 128):
                out_scr[q, f * 8 : (f + 1) * 8, :] = result[:, q * 128 : (q + 1) * 128]
        for b in range(n_blk):
            for lane in range(b * obs_blk, (b + 1) * obs_blk, 128):
                lanes = slice(lane, lane + 128)
                terms = [out_scr[lane // 128, pl.ds(t, NF, stride=8), :] for t in range(8)]
                x, y, z = (obs_ref[c : c + 1, lanes] for c in range(3))
                inner = slice(lane - b * obs_blk, lane - b * obs_blk + 128)
                press[b, 0:NF, inner] = terms[0] + x * terms[2] + y * terms[4] + z * terms[6]
                press[b, NF : 2 * NF, inner] = terms[1] + x * terms[3] + y * terms[5] + z * terms[7]

        def pressure_copy(i):
            to = device(lax.rem(me + i, devices))
            return pltpu.make_async_remote_copy(
                src_ref=press.at[to["blk"]],
                dst_ref=recv2.at[i],
                send_sem=send_sem2.at[i],
                recv_sem=recv_sem2.at[i],
                device_id=to,
                device_id_type=MESH,
            )

        each(devices, lambda i: pressure_copy(i).start())
        each(groups, lambda i: spectra_copy(i).wait_send())
        each(devices, lambda i: pressure_copy(i).wait_recv())
        if devices <= 16:
            total = press[blk]
            for i in range(1, devices):
                total += recv2[i]
        else:
            total = lax.fori_loop(1, devices, lambda i, s: s + recv2[i], press[blk])
        out_ref[...] = total
        each(devices, lambda i: pressure_copy(i).wait_send())

    scratch = [
        pltpu.VMEM((groups, 8 * NF, points), jnp.bfloat16),
        pltpu.VMEM((groups, 8 * NF, points), jnp.bfloat16),
        pltpu.VMEM((NF * 4 * points, n_obs), jnp.bfloat16),
        pltpu.VMEM((4 * points // 128, 8 * NF, 128), jnp.float32),
        pltpu.VMEM((n_obs // 128, 8 * NF, 128), jnp.float32),
        pltpu.VMEM((n_blk, 2 * NF, obs_blk), jnp.float32),
        pltpu.VMEM((devices, 2 * NF, obs_blk), jnp.float32),
        pltpu.SemaphoreType.DMA((groups,)),
        pltpu.SemaphoreType.DMA((groups,)),
        pltpu.SemaphoreType.DMA((devices,)),
        pltpu.SemaphoreType.DMA((devices,)),
    ]
    vmem = pl.BlockSpec(memory_space=pltpu.VMEM)
    return pl.pallas_call(
        kernel,
        out_shape=jax.ShapeDtypeStruct((2 * NF, obs_blk), jnp.float32),
        in_specs=[vmem, pl.BlockSpec(memory_space=pltpu.SMEM), vmem, vmem, vmem, vmem],
        out_specs=vmem,
        scratch_shapes=scratch,
        compiler_params=pltpu.CompilerParams(
            collective_id=0, has_side_effects=True, vmem_limit_bytes=56 * 2**20
        ),
    )


def local(cell_series, cell_count, cell_target, surface, observers):
    rows_dev, _, signal_readings = cell_series.shape
    points_dev = surface.shape[1]
    n_blk, n_split, n_sub = (lax.axis_size(a) for a in ("blk", "split", "sub"))
    devices = n_blk * n_split * n_sub
    amplitude = 150.0 * math.sqrt(
        signal_readings * points_dev / (rows_dev * (points_dev * devices))
    )
    twiddle = spectral_lookup_matrix(signal_readings)
    per_cell = jnp.einsum("jt,rct->cjr", twiddle, cell_series, preferred_element_type=jnp.float32)
    kernel = make_kernel(n_blk, n_split, n_sub, rows_dev, points_dev, observers.shape[1], amplitude)
    pressure = kernel(
        per_cell.reshape(8 * NF, rows_dev),
        cell_count,
        cell_target.reshape(1, rows_dev),
        surface,
        surface.T,
        observers,
    )
    return pressure.T.reshape(observers.shape[1] // n_blk, 2, NF)


def solution(mesh):
    return jax.shard_map(
        local,
        mesh=mesh,
        in_specs=(
            P(("case", "blk", "split", "sub"), None, None),
            P(("case", "blk", "split", "sub")),
            P(("case", "blk", "split", "sub")),
            P(None, ("case", "blk", "split", "sub")),
            P(None, "case"),
        ),
        out_specs=P(("case", "blk"), None, None),
        check_vma=False,
    )
```

time: 116 us -> 29.5 us (0.25)
  waiting for transfers between devices: 31.9 us -> 0 us
  other arithmetic: 30.6 us -> 0.2 us
  Pallas kernels: 0 us -> 22.2 us
  between operations: 14.3 us -> 0.67 us
  starting transfers between devices: 13.3 us -> 0 us
  local copies, waits for them, and re-layouts: 14.8 us -> 2.12 us
  blocking collectives: 6.44 us -> 0 us
    reduce_sum x9 -> x0, other arithmetic: 24.9 us -> none  [the longest x8 24.9 us: radiate(): jnp.sum(quadrature_factor * (source_real * cosine + source_imag * sinusoi...]
    pallas_call x0 -> x1, Pallas kernels: none -> 22.2 us  [local(): kernel(per_cell.reshape(8 * NF, rows_dev), cell_count, cell_target.reshap...]
    reduce_scatter x1 -> x0, waiting for transfers between devices: 18.1 us -> none  [local(): lax.psum_scatter(radiate(spectra, surface, observers, amplitude), 'blk',...]
    all_to_all x2 -> x0, waiting for transfers between devices: 13.8 us -> none  [the longest x1 13.8 us: local(): lax.all_to_all(outgoing.reshape(source_groups, capacity, 8 * NF), ('blk',...]
    all_to_all x2 -> x0, starting transfers between devices: 13.3 us -> none  [the longest x1 7.25 us: local(): lax.all_to_all(slot_point.reshape(source_groups, capacity), ('blk', 'spli...]
    gather x4 -> x0, local copies, waits for them, and re-layouts: 8.84 us -> none  [the longest x2 5.93 us: local(): slot_point = jnp.take(point_index, slot_source, mode='fill', fill_value=-1)]
    psum x1 -> x0, blocking collectives: 6.44 us -> none  [local(): return lax.psum(summed, ('split', 'sub'))]
    scatter x1 -> x0, local copies, waits for them, and re-layouts: 4.32 us -> none  [local(): jnp.full((slot_total + 1,), rows_dev, jnp.int32).at[destination]]
  transfers between devices with their start and end apart: 3 -> 0, of which waited for: 2 -> 0; matrix products, arithmetic and copies ran while one was open for 7% -> 0% of each run, Pallas kernels for 0% -> 0%
where the time goes in v1:
time: 29.5 us; the launch traced here: 29.3 us
  Pallas kernels  22.2 us (75%)
  matrix products  4.11 us (14%)
  local copies, waits for them, and re-layouts  2.12 us (7%)
  between operations  0.67 us (2%)
    pallas_call x1, Pallas kernels, local(): kernel(per_cell.reshape(8 * NF, rows_dev), cell_count, cell_target.reshap...  22.2 us
    dot_general x1, matrix products, local(): jnp.einsum('jt,rct->cjr', twiddle, cell_series, preferred_element_type=jn...  4.11 us
    unnamed x4, local copies, waits for them, and re-layouts  2.12 us

profile of v1, /device:TPU:0, one launch (start us, length us, event | category | flops | bytes accessed | tf_op | source)
XLA Modules:
  0.0 29.3 jit_solution(8624321027921375432)
XLA Ops:
  0.0 0.0 copy-start
  0.1 0.2 multiply_convert_fusion.1
  0.2 4.1 %fusion = f32[16,1024,4]{1,0,2:T(8,128)} fusion(bf16[1024,4,512]{2,1,0:T(4,128)(2,1)} %param.5, bf16[8,512]{1,0:T(8,128)(2,1)S(1)} %get-tuple-element.6, bf16[8,512]{1,0:T(8,128)(2,1)S(1)} %get-tuple-element.5), kind=kOutput, calls=%fused_computation | convolution fusion | flops 67141632 | bytes 4472832 | tf_op jit(solution)/shard_map/jt,rct->cjr/dot_general | solution.py:279
  4.3 0.0 copy-done
  4.3 0.8 %copy.7 = f32[4,256]{0,1:T(8,128)} copy(f32[4,256]{1,0:T(4,128)S(1)} %copy-done) | data formatting | bytes 8192 | tf_op args[3]
  5.8 22.2 %shard_map.55 = f32[16,128]{1,0:T(8,128)} custom-call(f32[64,1024]{1,0:T(8,128)} %bitcast.11, s32[1]{0:T(128)S(6)} %copy.11.count_ref, s32[1,1024]{1,0:T(1,128)} %bitcast.14, f32[4,256]{1,0:T(4,128)} %surface_ref.1, f32[256,4]{1,0:T(8,128)} %bitcast.12, f32[3,512]{1,0:T(4,128)} %obs_ref.1), custom_call_target="tpu_custom_call" | custom-call | tf_op jit(solution)/shard_map/pallas_call | solution.py:281
  28.0 1.3 %copy.12 = f32[128,2,8]{0,2,1:T(8,128)} copy(f32[128,2,8]{0,2,1:T(8,128)} %bitcast.13) | data formatting | bytes 16384
  (2 shorter events, 0.0 us)
Async XLA Ops:
  0.0 4.3 %copy-start = (f32[4,256]{1,0:T(4,128)S(1)}, f32[4,256]{1,0:T(4,128)}, u32[]{:S(2)}) copy-start(f32[4,256]{1,0:T(4,128)} %surface_ref.1) | copy-start | bytes 12292

commit v2 on v1

--- a/solution.py
+++ b/solution.py
@@ -53,7 +53,7 @@
 
 def make_kernel(n_blk, n_split, n_sub, rows, points, n_obs, amplitude):
     groups = n_blk * n_split
-    devices = groups * n_sub
+    places = n_split * n_sub
     obs_blk = n_obs // n_blk
     sin_c, cos_c = polynomials(7)
     half = 256 if n_obs % 256 == 0 else n_obs
@@ -63,28 +63,36 @@
         lax.fori_loop(1, count, lambda i, c: (body(i), c)[1], 0, unroll=count <= 16)
 
     def kernel(
-        pc_ref, count_ref, target_ref, surface_ref, surface_t_ref, obs_ref, out_ref,
-        stage, recv, green, rows_scr, out_scr, press, recv2,
-        send_sem, recv_sem, send_sem2, recv_sem2,
+        pc_ref, count_ref, target_ref, surface_ref, obs_ref, out_ref,
+        stage, recv, green, rows_scr, out_scr, press, recv2, recv3, surface_t_ref,
+        send_sem, recv_sem, send_sem2, recv_sem2, send_sem3, recv_sem3,
     ):
         blk = lax.axis_index("blk")
         split = lax.axis_index("split")
         sub = lax.axis_index("sub")
         group = blk * n_split + split
-        me = group * n_sub + sub
-
-        def device(index):
-            g = index // n_sub
-            return {"blk": g // n_split, "split": g % n_split, "sub": index % n_sub}
+        place = split * n_sub + sub
+
+        def group_device(i):
+            g = lax.rem(group + i, groups)
+            return {"blk": g // n_split, "split": lax.rem(g, n_split), "sub": sub}
+
+        def block_device(i):
+            return {"blk": lax.rem(blk + i, n_blk), "split": split, "sub": sub}
+
+        def place_device(i):
+            p = lax.rem(place + i, places)
+            return {"blk": blk, "split": p // n_sub, "sub": lax.rem(p, n_sub)}
 
         barrier = pltpu.get_barrier_semaphore()
 
-        def greet(i):
-            pl.semaphore_signal(
-                barrier, inc=1, device_id=device(lax.rem(me + i, devices)), device_id_type=MESH
-            )
-
-        each(devices, greet)
+        def greet(to):
+            pl.semaphore_signal(barrier, inc=1, device_id=to, device_id_type=MESH)
+
+        each(groups, lambda i: greet(group_device(i)))
+        for other in range(1, n_sub):
+            for at_split in range(n_split):
+                greet({"blk": blk, "split": at_split, "sub": lax.rem(sub + other, n_sub)})
 
         pc = pc_ref[...]
         high = pc.astype(jnp.bfloat16)
@@ -102,17 +110,16 @@
             return (sums[: 8 * NF] + sums[8 * NF :]).astype(jnp.bfloat16)
 
         def spectra_copy(i):
-            g = lax.rem(group + i, groups)
             return pltpu.make_async_remote_copy(
                 src_ref=stage.at[i],
                 dst_ref=recv.at[i],
                 send_sem=send_sem.at[i],
                 recv_sem=recv_sem.at[i],
-                device_id={"blk": g // n_split, "split": g % n_split, "sub": sub},
+                device_id=group_device(i),
                 device_id_type=MESH,
             )
 
-        pl.semaphore_wait(barrier, devices - 1)
+        pl.semaphore_wait(barrier, groups - 1 + n_split * (n_sub - 1))
 
         def send_spectra(i):
             stage[i] = partial_sums(lax.rem(group + i, groups))
@@ -120,6 +127,9 @@
 
         each(groups, send_spectra)
         stage[0] = partial_sums(group)
+
+        surface = surface_ref[...]
+        surface_t_ref[...] = jnp.concatenate([surface, surface], axis=0).T
 
         def green_step(step, carry):
             start = pl.multiple_of(step * step_q, step_q)
@@ -169,7 +179,6 @@
             spectra = lax.fori_loop(
                 1, groups, lambda i, s: s + recv[i].astype(jnp.float32), stage[0].astype(jnp.float32)
             )
-        surface = surface_ref[...]
         spectra = spectra * (surface[3:4] * (amplitude / (4.0 * math.pi)))
         wave = 0.5 + 0.25 * lax.broadcasted_iota(jnp.int32, (NF, points), 0).astype(jnp.float32)
         part = [
@@ -218,28 +227,43 @@
                 press[b, 0:NF, inner] = terms[0] + x * terms[2] + y * terms[4] + z * terms[6]
                 press[b, NF : 2 * NF, inner] = terms[1] + x * terms[3] + y * terms[5] + z * terms[7]
 
-        def pressure_copy(i):
-            to = device(lax.rem(me + i, devices))
+        def block_copy(i):
             return pltpu.make_async_remote_copy(
-                src_ref=press.at[to["blk"]],
+                src_ref=press.at[lax.rem(blk + i, n_blk)],
                 dst_ref=recv2.at[i],
                 send_sem=send_sem2.at[i],
                 recv_sem=recv_sem2.at[i],
-                device_id=to,
+                device_id=block_device(i),
                 device_id_type=MESH,
             )
 
-        each(devices, lambda i: pressure_copy(i).start())
+        def place_copy(i):
+            return pltpu.make_async_remote_copy(
+                src_ref=recv3.at[0],
+                dst_ref=recv3.at[i],
+                send_sem=send_sem3.at[i],
+                recv_sem=recv_sem3.at[i],
+                device_id=place_device(i),
+                device_id_type=MESH,
+            )
+
+        def summed(ref, count, first):
+            if count > 16:
+                return lax.fori_loop(1, count, lambda i, s: s + ref[i], first)
+            for i in range(1, count):
+                first += ref[i]
+            return first
+
+        each(n_blk, lambda i: block_copy(i).start())
         each(groups, lambda i: spectra_copy(i).wait_send())
-        each(devices, lambda i: pressure_copy(i).wait_recv())
-        if devices <= 16:
-            total = press[blk]
-            for i in range(1, devices):
-                total += recv2[i]
-        else:
-            total = lax.fori_loop(1, devices, lambda i, s: s + recv2[i], press[blk])
-        out_ref[...] = total
-        each(devices, lambda i: pressure_copy(i).wait_send())
+        each(n_blk, lambda i: block_copy(i).wait_recv())
+        total = summed(recv2, n_blk, press[blk])
+        recv3[0] = total
+        each(places, lambda i: place_copy(i).start())
+        each(n_blk, lambda i: block_copy(i).wait_send())
+        each(places, lambda i: place_copy(i).wait_recv())
+        out_ref[...] = summed(recv3, places, total)
+        each(places, lambda i: place_copy(i).wait_send())
 
     scratch = [
         pltpu.VMEM((groups, 8 * NF, points), jnp.bfloat16),
@@ -248,17 +272,21 @@
         pltpu.VMEM((4 * points // 128, 8 * NF, 128), jnp.float32),
         pltpu.VMEM((n_obs // 128, 8 * NF, 128), jnp.float32),
         pltpu.VMEM((n_blk, 2 * NF, obs_blk), jnp.float32),
-        pltpu.VMEM((devices, 2 * NF, obs_blk), jnp.float32),
+        pltpu.VMEM((n_blk, 2 * NF, obs_blk), jnp.float32),
+        pltpu.VMEM((places, 2 * NF, obs_blk), jnp.float32),
+        pltpu.VMEM((points, 8), jnp.float32),
         pltpu.SemaphoreType.DMA((groups,)),
         pltpu.SemaphoreType.DMA((groups,)),
-        pltpu.SemaphoreType.DMA((devices,)),
-        pltpu.SemaphoreType.DMA((devices,)),
+        pltpu.SemaphoreType.DMA((n_blk,)),
+        pltpu.SemaphoreType.DMA((n_blk,)),
+        pltpu.SemaphoreType.DMA((places,)),
+        pltpu.SemaphoreType.DMA((places,)),
     ]
     vmem = pl.BlockSpec(memory_space=pltpu.VMEM)
     return pl.pallas_call(
         kernel,
         out_shape=jax.ShapeDtypeStruct((2 * NF, obs_blk), jnp.float32),
-        in_specs=[vmem, pl.BlockSpec(memory_space=pltpu.SMEM), vmem, vmem, vmem, vmem],
+        in_specs=[vmem, pl.BlockSpec(memory_space=pltpu.SMEM), vmem, vmem, vmem],
         out_specs=vmem,
         scratch_shapes=scratch,
         compiler_params=pltpu.CompilerParams(
@@ -283,7 +311,6 @@
         cell_count,
         cell_target.reshape(1, rows_dev),
         surface,
-        surface.T,
         observers,
     )
     return pressure.T.reshape(observers.shape[1] // n_blk, 2, NF)

time: 29.5 us -> 30 us (1.017)
  Pallas kernels: 22.2 us -> 23.5 us
  local copies, waits for them, and re-layouts: 2.12 us -> 1.3 us
    pallas_call x1, Pallas kernels: 22.2 us -> 23.5 us  [local(): kernel(per_cell.reshape(8 * NF, rows_dev), cell_count, cell_target.reshap...]
    unnamed x4 -> x1, local copies, waits for them, and re-layouts: 2.12 us -> 1.3 us
where the time goes in v2:
time: 30 us; the launch traced here: 29.8 us
  Pallas kernels  23.5 us (78%)
  matrix products  4.11 us (14%)
  local copies, waits for them, and re-layouts  1.3 us (4%)
  between operations  0.67 us (2%)
    pallas_call x1, Pallas kernels, local(): kernel(per_cell.reshape(8 * NF, rows_dev), cell_count, cell_target.reshap...  23.5 us
    dot_general x1, matrix products, local(): jnp.einsum('jt,rct->cjr', twiddle, cell_series, preferred_element_type=jn...  4.11 us
    unnamed x1, local copies, waits for them, and re-layouts  1.3 us

profile of v2, /device:TPU:0, one launch (start us, length us, event | category | flops | bytes accessed | tf_op | source)
XLA Modules:
  0.0 29.8 jit_solution(5270326693314594296)
XLA Ops:
  0.1 0.2 multiply_convert_fusion.1
  0.2 4.1 %fusion = f32[16,1024,4]{1,0,2:T(8,128)} fusion(bf16[1024,4,512]{2,1,0:T(4,128)(2,1)} %param.5, bf16[8,512]{1,0:T(8,128)(2,1)S(1)} %get-tuple-element.6, bf16[8,512]{1,0:T(8,128)(2,1)S(1)} %get-tuple-element.5), kind=kOutput, calls=%fused_computation | convolution fusion | flops 67141632 | bytes 4472832 | tf_op jit(solution)/shard_map/jt,rct->cjr/dot_general | solution.py:307
  5.0 23.5 %shard_map.55 = f32[16,128]{1,0:T(8,128)} custom-call(f32[64,1024]{1,0:T(8,128)} %bitcast.10, s32[1]{0:T(128)S(6)} %copy.10.count_ref, s32[1,1024]{1,0:T(1,128)} %bitcast.12, f32[4,256]{1,0:T(4,128)} %surface_ref.1, f32[3,512]{1,0:T(4,128)} %obs_ref.1), custom_call_target="tpu_custom_call" | custom-call | tf_op jit(solution)/shard_map/pallas_call | solution.py:309
  28.5 1.3 %copy.11 = f32[128,2,8]{0,2,1:T(8,128)} copy(f32[128,2,8]{0,2,1:T(8,128)} %bitcast.11) | data formatting | bytes 16384
  (2 shorter events, 0.0 us)

commit v3 on v1

--- a/solution.py
+++ b/solution.py
@@ -51,7 +51,8 @@
     return total
 
 
-def make_kernel(n_blk, n_split, n_sub, rows, points, n_obs, amplitude):
+def make_kernel(n_blk, n_split, n_sub, rows, samples, points, n_obs, amplitude):
+    chunk = 128
     groups = n_blk * n_split
     devices = groups * n_sub
     obs_blk = n_obs // n_blk
@@ -59,13 +60,13 @@
     half = 256 if n_obs % 256 == 0 else n_obs
     step_q = 16
 
-    def each(count, body):
-        lax.fori_loop(1, count, lambda i, c: (body(i), c)[1], 0, unroll=count <= 16)
+    def each(count, body, first=1):
+        lax.fori_loop(first, count, lambda i, c: (body(i), c)[1], 0)
 
     def kernel(
-        pc_ref, count_ref, target_ref, surface_ref, surface_t_ref, obs_ref, out_ref,
-        stage, recv, green, rows_scr, out_scr, press, recv2,
-        send_sem, recv_sem, send_sem2, recv_sem2,
+        series_ref, twiddle_ref, count_ref, target_ref, surface_ref, obs_ref, out_ref,
+        series, per_cell, stage, recv, green, rows_scr, out_scr, press, recv2, surface_t_ref,
+        load_sem, send_sem, recv_sem, send_sem2, recv_sem2,
     ):
         blk = lax.axis_index("blk")
         split = lax.axis_index("split")
@@ -73,23 +74,54 @@
         group = blk * n_split + split
         me = group * n_sub + sub
 
-        def device(index):
-            g = index // n_sub
-            return {"blk": g // n_split, "split": g % n_split, "sub": index % n_sub}
+        def group_device(i):
+            g = lax.rem(group + i, groups)
+            return {"blk": g // n_split, "split": lax.rem(g, n_split), "sub": sub}
+
+        def any_device(i):
+            to = lax.rem(me + i, devices)
+            g = to // n_sub
+            return {"blk": g // n_split, "split": lax.rem(g, n_split), "sub": lax.rem(to, n_sub)}
+
+        def total(ref, count):
+            if count <= 16:
+                return sum(ref[i].astype(jnp.float32) for i in range(count))
+            zero = jnp.zeros(ref.shape[1:], jnp.float32)
+            return lax.fori_loop(0, count, lambda i, s: s + ref[i].astype(jnp.float32), zero)
+
+        def load(i):
+            cells = pl.ds(i * chunk, chunk)
+            return pltpu.make_async_copy(series_ref.at[cells], series.at[cells], load_sem.at[i])
+
+        each(rows // chunk, lambda i: load(i).start(), 0)
 
         barrier = pltpu.get_barrier_semaphore()
 
         def greet(i):
-            pl.semaphore_signal(
-                barrier, inc=1, device_id=device(lax.rem(me + i, devices)), device_id_type=MESH
-            )
+            pl.semaphore_signal(barrier, inc=1, device_id=any_device(i), device_id_type=MESH)
 
         each(devices, greet)
 
-        pc = pc_ref[...]
-        high = pc.astype(jnp.bfloat16)
-        low = (pc - high.astype(jnp.float32)).astype(jnp.bfloat16)
-        both = jnp.concatenate([high, low], axis=0)
+        twiddle = twiddle_ref[...]
+
+        def transform(i):
+            load(i).wait()
+            records = pl.ds(pl.multiple_of(4 * i * chunk, 4 * chunk), 4 * chunk)
+            per_cell[records, :] = lax.dot_general(
+                series[pl.ds(i * chunk, chunk)].reshape(4 * chunk, samples),
+                twiddle,
+                (((1,), (1,)), ((), ())),
+                preferred_element_type=jnp.float32,
+            )
+
+        each(rows // chunk, transform, 0)
+        lane = lax.broadcasted_iota(jnp.int32, (rows, 128), 1)
+        component = lane // (2 * NF) % 4
+        spectrum = per_cell[pl.ds(0, rows, stride=4), :]
+        for c in range(1, 4):
+            spectrum = jnp.where(component == c, per_cell[pl.ds(c, rows, stride=4), :], spectrum)
+        high = spectrum.astype(jnp.bfloat16).astype(jnp.float32)
+        both = jnp.where(lane < 8 * NF, high, spectrum - high).T.astype(jnp.bfloat16)
         live = lax.broadcasted_iota(jnp.int32, (1, rows), 1) < count_ref[0]
         target = jnp.where(live, target_ref[...], -1)
         point = lax.broadcasted_iota(jnp.int32, (points, rows), 0)
@@ -102,13 +134,12 @@
             return (sums[: 8 * NF] + sums[8 * NF :]).astype(jnp.bfloat16)
 
         def spectra_copy(i):
-            g = lax.rem(group + i, groups)
             return pltpu.make_async_remote_copy(
                 src_ref=stage.at[i],
                 dst_ref=recv.at[i],
                 send_sem=send_sem.at[i],
                 recv_sem=recv_sem.at[i],
-                device_id={"blk": g // n_split, "split": g % n_split, "sub": sub},
+                device_id=group_device(i),
                 device_id_type=MESH,
             )
 
@@ -119,7 +150,10 @@
             spectra_copy(i).start()
 
         each(groups, send_spectra)
-        stage[0] = partial_sums(group)
+        recv[0] = partial_sums(group)
+
+        surface = surface_ref[...]
+        surface_t_ref[...] = jnp.concatenate([surface, surface], axis=0).T
 
         def green_step(step, carry):
             start = pl.multiple_of(step * step_q, step_q)
@@ -161,15 +195,7 @@
         lax.fori_loop(0, points // step_q, green_step, 0)
 
         each(groups, lambda i: spectra_copy(i).wait_recv())
-        if groups <= 16:
-            spectra = stage[0].astype(jnp.float32)
-            for i in range(1, groups):
-                spectra += recv[i].astype(jnp.float32)
-        else:
-            spectra = lax.fori_loop(
-                1, groups, lambda i, s: s + recv[i].astype(jnp.float32), stage[0].astype(jnp.float32)
-            )
-        surface = surface_ref[...]
+        spectra = total(recv, groups)
         spectra = spectra * (surface[3:4] * (amplitude / (4.0 * math.pi)))
         wave = 0.5 + 0.25 * lax.broadcasted_iota(jnp.int32, (NF, points), 0).astype(jnp.float32)
         part = [
@@ -191,24 +217,23 @@
                     rows_scr[p * (points // 128) + q, t * NF : (t + 1) * NF, :] = value[
                         :, q * 128 : (q + 1) * 128
                     ]
-        for f in range(NF):
+
+        def radiate(f):
             left = jnp.concatenate(
-                [
-                    rows_scr[p, pl.ds(f, 8, stride=NF), :]
-                    for p in range(4 * points // 128)
-                ],
-                axis=1,
+                [rows_scr[p, pl.ds(f, 8, stride=NF), :] for p in range(4 * points // 128)], axis=1
             )
             left_high = left.astype(jnp.bfloat16).astype(jnp.float32)
             left = jnp.concatenate([left_high, left - left_high], axis=0).astype(jnp.bfloat16)
             result = jnp.dot(
                 left,
-                green[f * 4 * points : (f + 1) * 4 * points, :],
+                green[pl.ds(pl.multiple_of(f * 4 * points, 4 * points), 4 * points), :],
                 preferred_element_type=jnp.float32,
             )
             result = result[:8] + result[8:]
             for q in range(n_obs // 128):
-                out_scr[q, f * 8 : (f + 1) * 8, :] = result[:, q * 128 : (q + 1) * 128]
+                out_scr[q, pl.ds(pl.multiple_of(f * 8, 8), 8), :] = result[:, q * 128 : (q + 1) * 128]
+
+        each(NF, radiate, 0)
         for b in range(n_blk):
             for lane in range(b * obs_blk, (b + 1) * obs_blk, 128):
                 lanes = slice(lane, lane + 128)
@@ -219,7 +244,7 @@
                 press[b, NF : 2 * NF, inner] = terms[1] + x * terms[3] + y * terms[5] + z * terms[7]
 
         def pressure_copy(i):
-            to = device(lax.rem(me + i, devices))
+            to = any_device(i)
             return pltpu.make_async_remote_copy(
                 src_ref=press.at[to["blk"]],
                 dst_ref=recv2.at[i],
@@ -232,16 +257,13 @@
         each(devices, lambda i: pressure_copy(i).start())
         each(groups, lambda i: spectra_copy(i).wait_send())
         each(devices, lambda i: pressure_copy(i).wait_recv())
-        if devices <= 16:
-            total = press[blk]
-            for i in range(1, devices):
-                total += recv2[i]
-        else:
-            total = lax.fori_loop(1, devices, lambda i, s: s + recv2[i], press[blk])
-        out_ref[...] = total
+        recv2[0] = press[blk]
+        out_ref[...] = total(recv2, devices)
         each(devices, lambda i: pressure_copy(i).wait_send())
 
     scratch = [
+        pltpu.VMEM((rows, 4, samples), jnp.bfloat16),
+        pltpu.VMEM((4 * rows, 128), jnp.float32),
         pltpu.VMEM((groups, 8 * NF, points), jnp.bfloat16),
         pltpu.VMEM((groups, 8 * NF, points), jnp.bfloat16),
         pltpu.VMEM((NF * 4 * points, n_obs), jnp.bfloat16),
@@ -249,6 +271,8 @@
         pltpu.VMEM((n_obs // 128, 8 * NF, 128), jnp.float32),
         pltpu.VMEM((n_blk, 2 * NF, obs_blk), jnp.float32),
         pltpu.VMEM((devices, 2 * NF, obs_blk), jnp.float32),
+        pltpu.VMEM((points, 8), jnp.float32),
+        pltpu.SemaphoreType.DMA((rows // chunk,)),
         pltpu.SemaphoreType.DMA((groups,)),
         pltpu.SemaphoreType.DMA((groups,)),
         pltpu.SemaphoreType.DMA((devices,)),
@@ -258,7 +282,7 @@
     return pl.pallas_call(
         kernel,
         out_shape=jax.ShapeDtypeStruct((2 * NF, obs_blk), jnp.float32),
-        in_specs=[vmem, pl.BlockSpec(memory_space=pltpu.SMEM), vmem, vmem, vmem, vmem],
+        in_specs=[pl.BlockSpec(memory_space=pl.ANY), vmem, pl.BlockSpec(memory_space=pltpu.SMEM), vmem, vmem, vmem],
         out_specs=vmem,
         scratch_shapes=scratch,
         compiler_params=pltpu.CompilerParams(
@@ -276,14 +300,13 @@
         signal_readings * points_dev / (rows_dev * (points_dev * devices))
     )
     twiddle = spectral_lookup_matrix(signal_readings)
-    per_cell = jnp.einsum("jt,rct->cjr", twiddle, cell_series, preferred_element_type=jnp.float32)
-    kernel = make_kernel(n_blk, n_split, n_sub, rows_dev, points_dev, observers.shape[1], amplitude)
+    kernel = make_kernel(n_blk, n_split, n_sub, rows_dev, signal_readings, points_dev, observers.shape[1], amplitude)
     pressure = kernel(
-        per_cell.reshape(8 * NF, rows_dev),
+        cell_series,
+        jnp.concatenate([twiddle] * 8, axis=0),
         cell_count,
         cell_target.reshape(1, rows_dev),
         surface,
-        surface.T,
         observers,
     )
     return pressure.T.reshape(observers.shape[1] // n_blk, 2, NF)

time: 29.5 us -> 27.9 us (0.946)
  matrix products: 4.11 us -> 0 us
  other arithmetic: 0.2 us -> 2.49 us
  Pallas kernels: 22.2 us -> 23.1 us
  local copies, waits for them, and re-layouts: 2.12 us -> 1.3 us
    dot_general x1 -> x0, matrix products: 4.11 us -> none  [local(): jnp.einsum('jt,rct->cjr', twiddle, cell_series, preferred_element_type=jn...]
    unnamed x0 -> x15, other arithmetic: none -> 2.25 us
    pallas_call x1, Pallas kernels: 22.2 us -> 23.1 us  [local(): kernel(cell_series, jnp.concatenate([twiddle] * 8, axis=0), cell_count, c...]
    unnamed x4 -> x3, local copies, waits for them, and re-layouts: 2.12 us -> 1.3 us
where the time goes in v3:
time: 27.9 us; the launch traced here: 27.7 us
  Pallas kernels  23.1 us (83%)
  other arithmetic  2.49 us (9%)
  local copies, waits for them, and re-layouts  1.3 us (5%)
  between operations  0.74 us (3%)
    pallas_call x1, Pallas kernels, local(): kernel(cell_series, jnp.concatenate([twiddle] * 8, axis=0), cell_count, c...  23.1 us
    unnamed x15, other arithmetic  2.25 us
    unnamed x3, local copies, waits for them, and re-layouts  1.3 us

profile of v3, /device:TPU:0, one launch (start us, length us, event | category | flops | bytes accessed | tf_op | source)
XLA Modules:
  0.0 27.7 jit_solution(17517704654304363081)
XLA Ops:
  0.1 0.1 constant_dynamic-update-slice_fusion.15
  0.3 0.1 constant_dynamic-update-slice_fusion.14
  0.4 0.1 constant_dynamic-update-slice_fusion.13
  0.6 0.1 constant_dynamic-update-slice_fusion.12
  0.7 0.1 constant_dynamic-update-slice_fusion.11
  0.9 0.1 constant_dynamic-update-slice_fusion.10
  1.0 0.1 constant_dynamic-update-slice_fusion.9
  1.2 0.1 constant_dynamic-update-slice_fusion.8
  1.3 0.1 constant_dynamic-update-slice_fusion.7
  1.5 0.1 constant_dynamic-update-slice_fusion.6
  1.6 0.1 constant_dynamic-update-slice_fusion.5
  1.8 0.1 constant_dynamic-update-slice_fusion.4
  1.9 0.1 constant_dynamic-update-slice_fusion.3
  2.1 0.1 constant_dynamic-update-slice_fusion.2
  2.2 0.1 constant_dynamic-update-slice_fusion.1
  2.4 0.1 constant_dynamic-update-slice_fusion.twiddle_ref
  2.6 0.0 copy-start
  3.2 0.0 copy-done
  3.2 23.1 %shard_map.55 = f32[16,128]{1,0:T(8,128)} custom-call(bf16[1024,4,512]{2,1,0:T(4,128)(2,1)} %series_ref.1, bf16[128,512]{1,0:T(8,128)(2,1)} %copy-done, s32[1]{0:T(128)S(6)} %copy.22.count_ref, s32[1,1024]{1,0:T(1,128)} %bitcast.5, f32[4,256]{1,0:T(4,128)} %surface_ref.1, f32[3,512]{1,0:T(4,128)} %obs_ref.1), custom_call_target="tpu_custom_call" | custom-call | tf_op jit(solution)/shard_map/pallas_call | solution.py:304
  26.4 1.3 %copy.23 = f32[128,2,8]{0,2,1:T(8,128)} copy(f32[128,2,8]{0,2,1:T(8,128)} %bitcast.4) | data formatting | bytes 16384
  (3 shorter events, 0.1 us)
Async XLA Ops:
  2.6 0.7 %copy-start = (bf16[128,512]{1,0:T(8,128)(2,1)}, bf16[128,512]{1,0:T(8,128)(2,1)S(1)}, u32[]{:S(2)}) copy-start(bf16[128,512]{1,0:T(8,128)(2,1)S(1)} %constant_dynamic-update-slice_fusion.twiddle_ref) | copy-start | bytes 393220

commit v4 on v3

--- a/solution.py
+++ b/solution.py
@@ -2,6 +2,8 @@
 
 import jax
 import jax.numpy as jnp
+import ml_dtypes
+import numpy as np
 from jax import lax
 from jax.experimental import pallas as pl
 from jax.experimental.pallas import tpu as pltpu
@@ -12,8 +14,6 @@
 
 
 def polynomials(terms):
-    import numpy as np
-
     nodes = np.cos((np.arange(400) + 0.5) * np.pi / 400)
     squares = (nodes + 1.0) * 0.125
     u = np.sqrt(squares)
@@ -31,17 +31,15 @@
 
 
 def spectral_lookup_matrix(signal_readings):
-    clock_moments = jnp.arange(signal_readings, dtype=jnp.int32)
-    spectral_slot_number = jnp.arange(NF, dtype=jnp.int32) + signal_readings // 16
-    modulo_angle_value = spectral_slot_number[:, None] * clock_moments[None, :] % signal_readings
-    phases = 2.0 * math.pi / signal_readings * modulo_angle_value.astype(jnp.float32)
-    hann_attenuation_curve = 0.5 - 0.5 * jnp.cos(
-        2.0 * math.pi / signal_readings * clock_moments.astype(jnp.float32)
-    )
-    scaled = 2.0 / signal_readings * hann_attenuation_curve[None, :]
-    return jnp.concatenate([scaled * jnp.cos(phases), -scaled * jnp.sin(phases)], axis=0).astype(
-        jnp.bfloat16
-    )
+    moments = np.arange(signal_readings, dtype=np.int64)
+    slots = np.arange(NF, dtype=np.int64) + signal_readings // 16
+    modulo = slots[:, None] * moments[None, :] % signal_readings
+    step = np.float32(2.0 * math.pi / signal_readings)
+    phases = step * modulo.astype(np.float32)
+    hann = np.float32(0.5) - np.float32(0.5) * np.cos(step * moments.astype(np.float32))
+    scaled = np.float32(2.0 / signal_readings) * hann[None, :]
+    table = np.concatenate([scaled * np.cos(phases), -scaled * np.sin(phases)], axis=0)
+    return jnp.asarray(table.astype(ml_dtypes.bfloat16))
 
 
 def horner(coefficients, v):
@@ -93,16 +91,15 @@
             cells = pl.ds(i * chunk, chunk)
             return pltpu.make_async_copy(series_ref.at[cells], series.at[cells], load_sem.at[i])
 
-        each(rows // chunk, lambda i: load(i).start(), 0)
-
         barrier = pltpu.get_barrier_semaphore()
 
         def greet(i):
             pl.semaphore_signal(barrier, inc=1, device_id=any_device(i), device_id_type=MESH)
 
         each(devices, greet)
-
-        twiddle = twiddle_ref[...]
+        each(rows // chunk, lambda i: load(i).start(), 0)
+
+        twiddle = jnp.concatenate([twiddle_ref[...]] * 8, axis=0)
 
         def transform(i):
             load(i).wait()
@@ -303,7 +300,7 @@
     kernel = make_kernel(n_blk, n_split, n_sub, rows_dev, signal_readings, points_dev, observers.shape[1], amplitude)
     pressure = kernel(
         cell_series,
-        jnp.concatenate([twiddle] * 8, axis=0),
+        twiddle,
         cell_count,
         cell_target.reshape(1, rows_dev),
         surface,

time: 27.9 us -> 25.2 us (0.903)
  other arithmetic: 2.49 us -> 0 us
    unnamed x15 -> x0, other arithmetic: 2.25 us -> none
    unnamed x3 -> x1, local copies, waits for them, and re-layouts: 1.3 us -> 1.3 us
where the time goes in v4:
time: 25.2 us; the launch traced here: 24.9 us
  Pallas kernels  22.9 us (91%)
  local copies, waits for them, and re-layouts  1.3 us (5%)
  between operations  0.66 us (3%)
    pallas_call x1, Pallas kernels, local(): kernel(cell_series, twiddle, cell_count, cell_target.reshape(1, rows_dev)...  22.9 us
    unnamed x1, local copies, waits for them, and re-layouts  1.3 us

profile of v4, /device:TPU:0, one launch (start us, length us, event | category | flops | bytes accessed | tf_op | source)
XLA Modules:
  0.0 24.9 jit_solution(17405724143038864041)
XLA Ops:
  0.7 22.9 %shard_map.64 = f32[16,128]{1,0:T(8,128)} custom-call(bf16[1024,4,512]{2,1,0:T(4,128)(2,1)} %series_ref.1, bf16[16,512]{1,0:T(8,128)(2,1)} %constant.2.clone.twiddle_ref, s32[1]{0:T(128)S(6)} %copy.8.count_ref, s32[1,1024]{1,0:T(1,128)} %bitcast.5, f32[4,256]{1,0:T(4,128)} %surface_ref.1, f32[3,512]{1,0:T(4,128)} %obs_ref.1), custom_call_target="tpu_custom_call" | custom-call | tf_op jit(solution)/shard_map/pallas_call | solution.py:301
  23.6 1.3 %copy.9 = f32[128,2,8]{0,2,1:T(8,128)} copy(f32[128,2,8]{0,2,1:T(8,128)} %bitcast.4) | data formatting | bytes 16384

commit v5 on v4

--- a/solution.py
+++ b/solution.py
@@ -140,14 +140,17 @@
                 device_id_type=MESH,
             )
 
+
+        def far_first(n, count):
+            return count // 2 + (n // 2) * (2 * lax.rem(n, 2) - 1)
+
+        def fill(i):
+            stage[i] = partial_sums(lax.rem(group + i, groups))
+
+        each(groups, fill)
+        recv[0] = partial_sums(group)
         pl.semaphore_wait(barrier, devices - 1)
-
-        def send_spectra(i):
-            stage[i] = partial_sums(lax.rem(group + i, groups))
-            spectra_copy(i).start()
-
-        each(groups, send_spectra)
-        recv[0] = partial_sums(group)
+        each(groups, lambda n: spectra_copy(far_first(n, groups)).start())
 
         surface = surface_ref[...]
         surface_t_ref[...] = jnp.concatenate([surface, surface], axis=0).T
@@ -251,7 +254,7 @@
                 device_id_type=MESH,
             )
 
-        each(devices, lambda i: pressure_copy(i).start())
+        each(devices, lambda n: pressure_copy(far_first(n, devices)).start())
         each(groups, lambda i: spectra_copy(i).wait_send())
         each(devices, lambda i: pressure_copy(i).wait_recv())
         recv2[0] = press[blk]

time: 25.2 us -> 26.8 us (1.063)
  Pallas kernels: 22.9 us -> 24.5 us
    pallas_call x1, Pallas kernels: 22.9 us -> 24.5 us  [local(): kernel(cell_series, twiddle, cell_count, cell_target.reshape(1, rows_dev)...]
where the time goes in v5:
time: 26.8 us; the launch traced here: 26.5 us
  Pallas kernels  24.5 us (91%)
  local copies, waits for them, and re-layouts  1.3 us (5%)
  between operations  0.66 us (2%)
    pallas_call x1, Pallas kernels, local(): kernel(cell_series, twiddle, cell_count, cell_target.reshape(1, rows_dev)...  24.5 us
    unnamed x1, local copies, waits for them, and re-layouts  1.3 us

profile of v5, /device:TPU:0, one launch (start us, length us, event | category | flops | bytes accessed | tf_op | source)
XLA Modules:
  0.0 26.5 jit_solution(2894240762486804530)
XLA Ops:
  0.7 24.5 %shard_map.64 = f32[16,128]{1,0:T(8,128)} custom-call(bf16[1024,4,512]{2,1,0:T(4,128)(2,1)} %series_ref.1, bf16[16,512]{1,0:T(8,128)(2,1)} %constant.2.clone.twiddle_ref, s32[1]{0:T(128)S(6)} %copy.8.count_ref, s32[1,1024]{1,0:T(1,128)} %bitcast.5, f32[4,256]{1,0:T(4,128)} %surface_ref.1, f32[3,512]{1,0:T(4,128)} %obs_ref.1), custom_call_target="tpu_custom_call" | custom-call | tf_op jit(solution)/shard_map/pallas_call | solution.py:304
  25.2 1.3 %copy.9 = f32[128,2,8]{0,2,1:T(8,128)} copy(f32[128,2,8]{0,2,1:T(8,128)} %bitcast.4) | data formatting | bytes 16384
